TPU v7x, 128 devices: a whole 4x4x4 slice. The times are simulated.
128 devices in a mesh: dp: 4 (over x), expert: 8 (over z, core), tensor: 4 (over y).
Axes of the slice: x: 4, y: 4, z: 4, core: 2. Of those that a mesh axis runs over, the one named last changes fastest.
Arguments:
- tokens: bfloat16 [4096, 2048], P(('dp', 'expert')), may hold values from -6 to 6
- cotangent: bfloat16 [4096, 2048], P(('dp', 'expert')), may hold values from -6 to 6
- seq_lengths: int32 [32, 3], P(('dp', 'expert')), may hold values from 1 to 64, 128 in all within a row
- deal_order: int32 [4096], P(('dp', 'expert')), may hold values from 0 to 4095, as said below
- expert_ids: int32 [4096, 8], P(('dp', 'expert')), may hold values from 0 to 15, all different within a row
- slot_order: int32 [4096, 8], P(('dp', 'expert')), may hold values from 0 to 1023, as said below
- qkv_weight: bfloat16 [3, 2048, 2048], P(None, ('dp', 'expert'), 'tensor'), may hold values from -0.125 to 0.125
- out_weight: bfloat16 [2048, 2048], P('tensor', ('dp', 'expert')), may hold values from -0.5 to 0.5
- router_weight: bfloat16 [16, 2048], P(None, ('dp', 'expert')), may hold values from -0.0625 to 0.0625
- gate_weight: bfloat16 [16, 2048, 1024], P('expert', 'dp', 'tensor'), may hold values from -0.125 to 0.125
- up_weight: bfloat16 [16, 2048, 1024], P('expert', 'dp', 'tensor'), may hold values from -0.125 to 0.125
- down_weight: bfloat16 [16, 2048, 1024], P('expert', 'dp', 'tensor'), may hold values from -0.75 to 0.75
- gain_first: float32 [2048], replicated, may hold values from 0.5 to 1.5
- gain_second: float32 [2048], replicated, may hold values from 0.5 to 1.5
Outputs:
- layer_out: bfloat16 [4096, 2048], P(('dp', 'expert'), 'tensor')
- input_grad: bfloat16 [4096, 2048], P(('dp', 'expert'), 'tensor')
- qkv_grad: float32 [3, 2048, 2048], P(None, ('dp', 'expert'), 'tensor')
- out_grad: float32 [2048, 2048], P('tensor', ('dp', 'expert'))
- router_grad: float32 [16, 2048], P(None, ('dp', 'expert'))
- gate_grad: float32 [16, 2048, 1024], P('expert', 'dp', 'tensor')
- up_grad: float32 [16, 2048, 1024], P('expert', 'dp', 'tensor')
- down_grad: float32 [16, 2048, 1024], P('expert', 'dp', 'tensor')
- gain_first_grad: float32 [2048], P(('dp', 'expert'))
- gain_second_grad: float32 [2048], P(('dp', 'expert'))
Inputs may be any that keep to these rules, and one draw needn't show every extreme that they name: `deal_order`: A permutation of the token rows. Row t of group g = t // 128 is dealt to a group d with d // 8 == g // 8, at a position from d * 128 + (g % 8) * 16 up to 16 more; each such block of 16 positions is filled from group g exactly. `slot_order`: in each aligned block of 128 rows the 1024 entries are a permutation. `seq_lengths`: each row sums to 128. `expert_ids`: each row names 8 different experts.
All inputs are finite; a program needn't handle non-finite values.
Results may differ from a plain program's by a relative error of at most 0.023.
Values may be sent and summed in bfloat16 or wider, within the bound.
No kernel may reach another device: no remote copies, remote signals or barrier semaphores. Data moves between devices by JAX's collectives and lax.ppermute only.
A program may use at most 128 MiB of HBM per device.

v0:
```python
import jax
import jax.numpy as jnp
from jax import lax
from jax.sharding import PartitionSpec as P

HEAD_DIM = 128


EPSILON = 1e-05


def segment_of(seq_lengths, row_count):
    seq_ends = jnp.cumsum(seq_lengths)
    position = jnp.arange(row_count, dtype=jnp.int32)
    return jnp.sum((position[:, None] >= seq_ends[None, :]).astype(jnp.int32), axis=1)


def slot_targets(chosen, pair_order, experts, capacity):
    flat_ids = chosen.reshape(-1)
    flat_order = pair_order.reshape(-1)
    pair_count = flat_ids.shape[0]
    by_rank = (
        jnp.zeros((pair_count,), jnp.int32)
        .at[flat_order]
        .set(jnp.arange(pair_count, dtype=jnp.int32))
    )
    ranked_ids = flat_ids[by_rank]
    expert_match = (ranked_ids[:, None] == jnp.arange(experts, dtype=jnp.int32)[None, :]).astype(
        jnp.int32
    )
    earlier = jnp.cumsum(expert_match, axis=0) - expert_match
    ranked_slot = jnp.sum(earlier * expert_match, axis=1)
    slot_index = jnp.zeros((pair_count,), jnp.int32).at[by_rank].set(ranked_slot)
    slot_target = jnp.where(
        slot_index < capacity, flat_ids * capacity + slot_index, experts * capacity
    )
    return slot_target.reshape(chosen.shape)


def column_part(values, part_count, part_index):
    piece = values.shape[-1] // part_count
    return lax.dynamic_slice_in_dim(values, part_index * piece, piece, values.ndim - 1)


def head_total(partial_rows):
    return lax.psum(partial_rows, "tensor")


def whole_move(buffer):
    return lax.all_to_all(buffer, "expert", split_axis=0, concat_axis=0, tiled=True)


def share_sum(terms):
    return lax.psum_scatter(
        terms.astype(jnp.bfloat16), "tensor", scatter_dimension=3, tiled=True
    ).astype(jnp.float32)


def share_return(rows):
    return lax.all_to_all(rows, "expert", split_axis=0, concat_axis=0, tiled=True)


def to_experts(buffer):
    return whole_move(buffer)


def local(
    tokens,
    cotangent,
    seq_lengths,
    deal_order,
    expert_ids,
    slot_order,
    qkv_weight,
    out_weight,
    router_weight,
    gate_weight,
    up_weight,
    down_weight,
    gain_first,
    gain_second,
):
    rows_grp, model_width = tokens.shape
    peer_count = lax.axis_size("expert")
    peer_rows = rows_grp // peer_count
    sender_index = lax.axis_index("expert")
    part_count = lax.axis_size("tensor")
    part_index = lax.axis_index("tensor")
    dest_group = deal_order // rows_grp % peer_count
    dealt_place = dest_group * peer_rows + (deal_order % rows_grp - sender_index * peer_rows)
    send_rows = (
        jnp.zeros_like(tokens)
        .at[dealt_place]
        .set(tokens)
        .reshape(peer_count, peer_rows, model_width)
    )
    send_grad = (
        jnp.zeros_like(cotangent)
        .at[dealt_place]
        .set(cotangent)
        .reshape(peer_count, peer_rows, model_width)
    )
    got_rows, got_grad = (
        lax.all_to_all(send_rows, "expert", split_axis=0, concat_axis=0, tiled=True),
        lax.all_to_all(send_grad, "expert", split_axis=0, concat_axis=0, tiled=True),
    )
    resid_in = got_rows.reshape(rows_grp, model_width).astype(jnp.float32)
    upstream = got_grad.reshape(rows_grp, model_width).astype(jnp.float32)
    qkv_full, out_full, router_full = (
        lax.all_gather(qkv_weight, ("dp", "expert"), axis=1, tiled=True),
        lax.all_gather(out_weight, ("dp", "expert"), axis=1, tiled=True),
        lax.all_gather(router_weight, ("dp", "expert"), axis=1, tiled=True),
    )
    gate_full, up_full, down_full = (
        lax.all_gather(gate_weight, "dp", axis=1, tiled=True),
        lax.all_gather(up_weight, "dp", axis=1, tiled=True),
        lax.all_gather(down_weight, "dp", axis=1, tiled=True),
    )
    experts = router_full.shape[0]
    top_count = expert_ids.shape[1]
    capacity = (5 * rows_grp * top_count + 4 * experts - 1) // (4 * experts)
    local_experts = gate_full.shape[0]
    head_width = qkv_full.shape[2]
    heads_here = head_width // HEAD_DIM
    score_scale = HEAD_DIM ** (-0.5)
    factor_first = lax.rsqrt(jnp.mean(resid_in * resid_in, axis=-1, keepdims=True) + EPSILON)
    unit_first = resid_in * factor_first
    normed = (unit_first * gain_first).astype(jnp.bfloat16)
    projected = jnp.einsum(
        "td,sdj->stj", normed, qkv_full, preferred_element_type=jnp.float32
    ).astype(jnp.bfloat16)
    queries = projected[0].reshape(rows_grp, heads_here, HEAD_DIM)
    keys_here = projected[1].reshape(rows_grp, heads_here, HEAD_DIM)
    values_here = projected[2].reshape(rows_grp, heads_here, HEAD_DIM)
    segment = segment_of(seq_lengths[0], rows_grp)
    same_seq = (segment[:, None] == segment[None, :])[None, :, :]
    raw_scores = (
        jnp.einsum("qhd,khd->hqk", queries, keys_here, preferred_element_type=jnp.float32)
        * score_scale
    )
    scores = jnp.where(same_seq, raw_scores, -1000000000.0)
    row_peak = jnp.max(scores, axis=-1, keepdims=True)
    exponent = jnp.exp(scores - row_peak)
    row_total = jnp.sum(exponent, axis=-1, keepdims=True)
    weights = exponent / row_total
    log_total = row_peak + jnp.log(row_total)
    mixed_heads = jnp.einsum(
        "hqk,khd->qhd",
        weights.astype(jnp.bfloat16),
        values_here,
        preferred_element_type=jnp.float32,
    )
    mixed_heads = mixed_heads.astype(jnp.bfloat16).reshape(rows_grp, head_width)
    resid = resid_in + head_total(
        jnp.dot(mixed_heads, out_full, preferred_element_type=jnp.float32)
    )
    factor_second = lax.rsqrt(jnp.mean(resid * resid, axis=-1, keepdims=True) + EPSILON)
    unit_second = resid * factor_second
    hidden = (unit_second * gain_second).astype(jnp.bfloat16)
    router_logits = jnp.einsum("td,ed->te", hidden, router_full, preferred_element_type=jnp.float32)
    picked_logits = jnp.take_along_axis(router_logits, expert_ids, axis=1)
    gate_values = jax.nn.softmax(picked_logits, axis=-1)
    slot_target = slot_targets(expert_ids, slot_order, experts, capacity)
    flat_target = slot_target.reshape(-1)
    pair_rows = jnp.broadcast_to(hidden[:, None, :], (rows_grp, top_count, model_width)).reshape(
        -1, model_width
    )
    buffer = (
        jnp.zeros((experts * capacity + 1, model_width), jnp.bfloat16)
        .at[flat_target]
        .set(pair_rows)
    )
    arrived = to_experts(buffer[:-1].reshape(peer_count, local_experts, capacity, model_width))
    gate_part = jnp.einsum("secd,edf->secf", arrived, gate_full, preferred_element_type=jnp.float32)
    up_part = jnp.einsum("secd,edf->secf", arrived, up_full, preferred_element_type=jnp.float32)
    sigmoid_gate = jax.nn.sigmoid(gate_part)
    silu_gate = gate_part * sigmoid_gate
    active = (silu_gate * up_part).astype(jnp.bfloat16)
    expert_out = jnp.einsum("secf,edf->secd", active, down_full, preferred_element_type=jnp.float32)
    summed = share_sum(expert_out)
    returned = share_return(summed.astype(jnp.bfloat16))
    narrow = returned.shape[3]
    back_table = jnp.concatenate(
        [returned.reshape(-1, narrow), jnp.zeros((1, narrow), jnp.bfloat16)], axis=0
    )
    picked = back_table[slot_target].astype(jnp.float32)
    resid_part = column_part(resid, part_count, part_index)
    output_part = (resid_part + jnp.sum(gate_values[:, :, None] * picked, axis=1)).astype(
        jnp.bfloat16
    )
    upstream_part = column_part(upstream, part_count, part_index)
    gate_dot_part = jnp.sum(upstream_part[:, None, :] * picked, axis=-1)
    grad_rows = (
        (gate_values[:, :, None] * upstream[:, None, :])
        .astype(jnp.bfloat16)
        .reshape(-1, model_width)
    )
    grad_buffer = (
        jnp.zeros((experts * capacity + 1, model_width), jnp.bfloat16)
        .at[flat_target]
        .set(grad_rows)
    )
    grad_arrived = to_experts(
        grad_buffer[:-1].reshape(peer_count, local_experts, capacity, model_width)
    )
    grad_active = jnp.einsum(
        "secd,edf->secf", grad_arrived, down_full, preferred_element_type=jnp.float32
    )
    grad_down = jnp.einsum(
        "secf,secd->edf", active, grad_arrived, preferred_element_type=jnp.float32
    )
    grad_gate = (
        grad_active * up_part * sigmoid_gate * (1.0 + gate_part * (1.0 - sigmoid_gate))
    ).astype(jnp.bfloat16)
    grad_up = (grad_active * silu_gate).astype(jnp.bfloat16)
    grad_gate_w = jnp.einsum(
        "secd,secf->edf", arrived, grad_gate, preferred_element_type=jnp.float32
    )
    grad_up_w = jnp.einsum("secd,secf->edf", arrived, grad_up, preferred_element_type=jnp.float32)
    grad_sent = jnp.einsum(
        "secf,edf->secd", grad_gate, gate_full, preferred_element_type=jnp.float32
    )
    grad_sent = grad_sent + jnp.einsum(
        "secf,edf->secd", grad_up, up_full, preferred_element_type=jnp.float32
    )
    grad_sent, gate_dots = lax.psum((grad_sent, gate_dot_part), "tensor")
    grad_back = whole_move(grad_sent.astype(jnp.bfloat16))
    grad_table = jnp.concatenate(
        [grad_back.reshape(-1, model_width), jnp.zeros((1, model_width), jnp.bfloat16)], axis=0
    )
    grad_hidden = jnp.sum(grad_table[slot_target].astype(jnp.float32), axis=1)
    grad_picked = gate_values * (
        gate_dots - jnp.sum(gate_dots * gate_values, axis=-1, keepdims=True)
    )
    expert_match = (
        expert_ids[:, :, None] == jnp.arange(experts, dtype=jnp.int32)[None, None, :]
    ).astype(jnp.float32)
    grad_logits = jnp.sum(grad_picked[:, :, None] * expert_match, axis=1).astype(jnp.bfloat16)
    grad_hidden = grad_hidden + jnp.dot(
        grad_logits, router_full, preferred_element_type=jnp.float32
    )
    grad_router = jnp.einsum("te,td->ed", grad_logits, hidden, preferred_element_type=jnp.float32)
    grad_gain_second = jnp.sum(grad_hidden * unit_second, axis=0)
    scaled = grad_hidden * gain_second
    grad_resid = upstream + factor_second * (
        scaled - unit_second * jnp.mean(scaled * unit_second, axis=-1, keepdims=True)
    )
    grad_branch = grad_resid.astype(jnp.bfloat16)
    grad_out_w = jnp.einsum(
        "tj,td->jd", mixed_heads, grad_branch, preferred_element_type=jnp.float32
    )
    grad_mixed = jnp.einsum("td,jd->tj", grad_branch, out_full, preferred_element_type=jnp.float32)
    grad_mixed = grad_mixed.astype(jnp.bfloat16).reshape(rows_grp, heads_here, HEAD_DIM)
    again_scores = (
        jnp.einsum("qhd,khd->hqk", queries, keys_here, preferred_element_type=jnp.float32)
        * score_scale
    )
    weights_again = jnp.exp(jnp.where(same_seq, again_scores, -1000000000.0) - log_total)
    grad_values = jnp.einsum(
        "hqk,qhd->khd",
        weights_again.astype(jnp.bfloat16),
        grad_mixed,
        preferred_element_type=jnp.float32,
    ).astype(jnp.bfloat16)
    grad_weights = jnp.einsum(
        "qhd,khd->hqk", grad_mixed, values_here, preferred_element_type=jnp.float32
    )
    offset = jnp.sum(grad_weights * weights_again, axis=-1, keepdims=True)
    grad_scores = (weights_again * (grad_weights - offset)).astype(jnp.bfloat16)
    grad_queries = (
        jnp.einsum("hqk,khd->qhd", grad_scores, keys_here, preferred_element_type=jnp.float32)
        * score_scale
    ).astype(jnp.bfloat16)
    grad_keys = (
        jnp.einsum("hqk,qhd->khd", grad_scores, queries, preferred_element_type=jnp.float32)
        * score_scale
    ).astype(jnp.bfloat16)
    grad_proj = jnp.stack(
        [
            grad_queries.reshape(rows_grp, head_width),
            grad_keys.reshape(rows_grp, head_width),
            grad_values.reshape(rows_grp, head_width),
        ]
    )
    grad_normed = head_total(
        jnp.einsum("stj,sdj->td", grad_proj, qkv_full, preferred_element_type=jnp.float32)
    )
    grad_qkv = jnp.einsum("td,stj->sdj", normed, grad_proj, preferred_element_type=jnp.float32)
    grad_gain_first = jnp.sum(grad_normed * unit_first, axis=0)
    scaled_first = grad_normed * gain_first
    grad_input = grad_resid + factor_first * (
        scaled_first - unit_first * jnp.mean(scaled_first * unit_first, axis=-1, keepdims=True)
    )
    gain_terms = jnp.stack([grad_gain_first, grad_gain_second])
    qkv_grad, out_grad, router_grad, gain_grads = (
        lax.psum_scatter(
            grad_qkv.astype(jnp.bfloat16), ("dp", "expert"), scatter_dimension=1, tiled=True
        ).astype(jnp.float32),
        lax.psum_scatter(
            grad_out_w.astype(jnp.bfloat16), ("dp", "expert"), scatter_dimension=1, tiled=True
        ).astype(jnp.float32),
        lax.psum_scatter(
            grad_router.astype(jnp.bfloat16), ("dp", "expert"), scatter_dimension=1, tiled=True
        ).astype(jnp.float32),
        lax.psum_scatter(
            gain_terms.astype(jnp.bfloat16), ("dp", "expert"), scatter_dimension=1, tiled=True
        ).astype(jnp.float32),
    )
    gate_grad, up_grad, down_grad = (
        lax.psum_scatter(
            grad_gate_w.astype(jnp.bfloat16), "dp", scatter_dimension=1, tiled=True
        ).astype(jnp.float32),
        lax.psum_scatter(
            grad_up_w.astype(jnp.bfloat16), "dp", scatter_dimension=1, tiled=True
        ).astype(jnp.float32),
        lax.psum_scatter(
            grad_down.astype(jnp.bfloat16), "dp", scatter_dimension=1, tiled=True
        ).astype(jnp.float32),
    )
    input_part = column_part(grad_input, part_count, part_index).astype(jnp.bfloat16)
    back_out, back_input = (
        lax.all_to_all(
            output_part.reshape(peer_count, peer_rows, narrow),
            "expert",
            split_axis=0,
            concat_axis=0,
            tiled=True,
        ),
        lax.all_to_all(
            input_part.reshape(peer_count, peer_rows, narrow),
            "expert",
            split_axis=0,
            concat_axis=0,
            tiled=True,
        ),
    )
    final_out = back_out.reshape(rows_grp, narrow)[dealt_place]
    final_input = back_input.reshape(rows_grp, narrow)[dealt_place]
    return (
        final_out,
        final_input,
        qkv_grad,
        out_grad,
        router_grad,
        gate_grad,
        up_grad,
        down_grad,
        gain_grads[0],
        gain_grads[1],
    )


def solution(mesh):
    placed = (
        P(("dp", "expert"), None),
        P(("dp", "expert"), None),
        P(("dp", "expert"), None),
        P(("dp", "expert")),
        P(("dp", "expert"), None),
        P(("dp", "expert"), None),
        P(None, ("dp", "expert"), "tensor"),
        P("tensor", ("dp", "expert")),
        P(None, ("dp", "expert")),
        P("expert", "dp", "tensor"),
        P("expert", "dp", "tensor"),
        P("expert", "dp", "tensor"),
        P(),
        P(),
    )
    return jax.shard_map(
        local,
        mesh=mesh,
        in_specs=placed,
        out_specs=(
            P(("dp", "expert"), "tensor"),
            P(("dp", "expert"), "tensor"),
            P(None, ("dp", "expert"), "tensor"),
            P("tensor", ("dp", "expert")),
            P(None, ("dp", "expert")),
            P("expert", "dp", "tensor"),
            P("expert", "dp", "tensor"),
            P("expert", "dp", "tensor"),
            P(("dp", "expert")),
            P(("dp", "expert")),
        ),
        check_vma=False,
    )
```

profile of v0, /device:TPU:0, one launch (start us, length us, event | category | flops | bytes accessed | tf_op | source)
XLA Modules:
  0.0 1218.1 jit_solution(215179281699254351)
XLA Ops:
  19.3 10.2 all-to-all-done
  31.7 32.3 %all-gather.7.cloned.1.call-done = bf16[3,2048,512]{2,1,0:T(8,128)(2,1)} async-done(((bf16[3,64,512]{2,1,0:T(8,128)(2,1)}), bf16[3,2048,512]{2,1,0:T(8,128)(2,1)}) %all-gather.7.cloned.1.call-update) | async-done | bytes 6291472 | tf_op jit(solution)/shard_map/all_gather | solution.py:110
  69.4 39.8 %all-gather.9.cloned.1.call-done = bf16[512,2048]{0,1:T(8,128)(2,1)} async-done(((bf16[512,64]{0,1:T(8,128)(2,1)}), bf16[512,2048]{0,1:T(8,128)(2,1)}) %all-gather.9.cloned.1.call-update) | async-done | bytes 2097168 | tf_op jit(solution)/shard_map/all_gather | solution.py:111
  138.3 19.8 %all-reduce.9.cloned.1.call-done = f32[128,2048]{1,0:T(8,128)} async-done(((f32[128,2048]{1,0:T(8,128)}), f32[128,2048]{1,0:T(8,128)}) %all-reduce.9.cloned.1.call-update) | async-done | bytes 1048592 | tf_op jit(solution)/shard_map/psum | solution.py:46
  159.7 9.6 scatter_custom_fusion.3
  169.3 5.7 slice.53
  181.3 74.8 %all-gather = bf16[32,64,16]{1,2,0:T(8,128)(2,1)S(1)} all-gather(bf16[1,64,16]{1,2,0:T(8,128)(2,1)S(1)} %bitcast.208), channel_id=1, replica_groups=mesh['dp'=4,'expert'=8,'tensor'=4] {'dp','expert'}, dimensions={0}, use_global_device_ids=true | all-gather | bytes 67584 | tf_op jit(solution)/shard_map/all_gather | solution.py:112
  257.8 7.0 gather_fusion.5
  265.3 10.0 scatter_custom_fusion.5
  275.3 5.7 slice.54
  286.8 5.8 fusion.30
  292.5 5.7 fusion.25
  298.3 20.9 %all-gather.15.cloned.1.call-done = bf16[2,2048,256]{2,1,0:T(8,128)(2,1)} async-done(((bf16[2,512,256]{2,1,0:T(8,128)(2,1)}), bf16[2,2048,256]{2,1,0:T(8,128)(2,1)}) %all-gather.15.cloned.1.call-update) | async-done | bytes 2097168 | tf_op jit(solution)/shard_map/all_gather | solution.py:117
  319.1 27.5 %all-to-all-done.5 = bf16[8,2,80,2048]{3,2,1,0:T(8,128)(2,1)} async-done(((bf16[8,2,80,2048]{3,2,1,0:T(8,128)(2,1)}), bf16[8,2,80,2048]{3,2,1,0:T(8,128)(2,1)}, u32[]{:S(2)}, u32[]{:S(2)}) %all-to-all-start.5) | async-done | bytes 5242912 | tf_op jit(solution)/shard_map/all_to_all | solution.py:50
  346.6 7.0 multiply_convert_fusion
  359.5 52.7 %reduce-scatter.12.cloned.1.call-done = bf16[8,2,80,512]{3,2,0,1:T(8,128)(2,1)} async-done(((bf16[8,2,80,2048]{3,2,0,1:T(8,128)(2,1)}), bf16[8,2,80,512]{3,2,0,1:T(8,128)(2,1)}) %reduce-scatter.12.cloned.1.call-update) | async-done | bytes 1310736 | tf_op jit(solution)/shard_map/reduce_scatter | solution.py:54
  428.2 9.7 all-to-all-done.2
  448.6 182.2 %all-reduce.14 = (bf16[8,2,80,2048]{3,2,0,1:T(8,128)(2,1)}, f32[128,8]{0,1:T(8,128)S(1)}) all-reduce(f32[8,2,80,2048]{3,2,0,1:T(8,128)} %add_bitcast_fusion, f32[128,8]{0,1:T(8,128)S(1)} %copy.229), channel_id=1, replica_groups=mesh['dp'=4,'expert'=8,'tensor'=4] {'tensor'}, use_global_device_ids=true, to_apply=%region_20.21 | all-reduce | flops 2622464 | bytes 15736832 | tf_op jit(solution)/shard_map/psum | solution.py:226
  642.0 60.2 %all-to-all-done.6 = bf16[8,2,80,2048]{3,2,1,0:T(8,128)(2,1)} async-done(((bf16[8,2,80,2048]{3,2,1,0:T(8,128)(2,1)}), bf16[8,2,80,2048]{3,2,1,0:T(8,128)(2,1)}, u32[]{:S(2)}, u32[]{:S(2)}) %all-to-all-start.6) | async-done | bytes 5242912 | tf_op jit(solution)/shard_map/all_to_all | solution.py:50
  702.1 5.7 concatenate.7
  707.8 12.0 gather_fusion.3
  738.4 5.9 convolution_bitcast_fusion
  744.6 6.3 bitcast_convert_fusion
  750.9 6.4 bitcast_convert_fusion.1
  757.4 6.7 bitcast_convert_fusion.2
  767.6 21.3 %all-reduce.11.cloned.1.call-done = f32[128,2048]{1,0:T(8,128)} async-done(((f32[128,2048]{1,0:T(8,128)}), f32[128,2048]{1,0:T(8,128)}) %all-reduce.11.cloned.1.call-update) | async-done | bytes 1048592 | tf_op jit(solution)/shard_map/psum | solution.py:46
  798.4 14.2 %copy.246 = bf16[3,2048,512]{2,0,1:T(4,128)(2,1)} copy(bf16[3,2048,512]{1,2,0:T(8,128)(2,1)} %convert_bitcast_fusion) | data formatting | bytes 12582912 | tf_op jit(solution)/shard_map/convert_element_type | solution.py:297
  826.2 16.6 %reduce-scatter.16.cloned.1.call-done = bf16[2,512,256]{2,1,0:T(8,128)(2,1)} async-done(((bf16[2,2048,256]{2,1,0:T(8,128)(2,1)}), bf16[2,512,256]{2,1,0:T(8,128)(2,1)}) %reduce-scatter.16.cloned.1.call-update) | async-done | bytes 524304 | tf_op jit(solution)/shard_map/reduce_scatter | solution.py:310
  844.9 78.6 %reduce-scatter.22.cloned.1.call-done = bf16[64,16]{1,0:T(8,128)(2,1)} async-done(((bf16[2048,16]{1,0:T(8,128)(2,1)}), bf16[64,16]{1,0:T(8,128)(2,1)}) %reduce-scatter.22.cloned.1.call-update) | async-done | bytes 2064
  932.1 71.5 %reduce-scatter.24.cloned.1.call-done = bf16[64,2]{1,0:T(8,128)(2,1)} async-done(((bf16[2048,2]{1,0:T(8,128)(2,1)}), bf16[64,2]{1,0:T(8,128)(2,1)}) %reduce-scatter.24.cloned.1.call-update) | async-done | bytes 272
  1006.4 120.9 %all-reduce.13.cloned.1.call-done = bf16[3,2048,512]{2,0,1:T(4,128)(2,1)} async-done(((bf16[3,2048,512]{2,0,1:T(4,128)(2,1)}), bf16[3,2048,512]{2,0,1:T(4,128)(2,1)}) %all-reduce.13.cloned.1.call-update) | async-done | bytes 6291472
  1129.2 80.0 %reduce-scatter.14.cloned.1.call-done = bf16[512,64]{0,1:T(8,128)(2,1)} async-done(((bf16[512,2048]{0,1:T(8,128)(2,1)}), bf16[512,64]{0,1:T(8,128)(2,1)}) %reduce-scatter.14.cloned.1.call-update) | async-done | bytes 65552 | tf_op jit(solution)/shard_map/reduce_scatter | solution.py:299
  (253 shorter events, 168.4 us)
Async XLA Ops:
  8.0 56.0 %all-gather.7.cloned.1.call-start = ((), (), s32[]{:S(2)}) async-start(), calls=%async_computation.15 | async-start | bytes 6488064 | tf_op jit(solution)/shard_map/all_gather | solution.py:110
  8.7 100.4 %all-gather.9.cloned.1.call-start = ((), (), s32[]{:S(2)}) async-start(), calls=%async_computation.16 | async-start | bytes 2162688 | tf_op jit(solution)/shard_map/all_gather | solution.py:111
  10.2 102.4 %copy-start.41 = (s32[128]{0:T(128)}, s32[128]{0:T(128)S(1)}, u32[]{:S(2)}) copy-start(s32[128]{0:T(128)S(1)} %compare_select_fusion.5) | copy-start | bytes 1540
  12.8 16.6 %all-to-all-start = ((bf16[8,16,2048]{2,1,0:T(8,128)(2,1)}), bf16[8,16,2048]{2,1,0:T(8,128)(2,1)S(1)}, u32[]{:S(2)}, u32[]{:S(2)}) async-start(bf16[8,16,2048]{2,1,0:T(8,128)(2,1)} %bitcast), calls=%async_computation | async-start | bytes 1048576 | tf_op jit(solution)/shard_map/all_to_all | solution.py:104
  18.2 139.8 %all-reduce.9.cloned.1.call-start = ((), (), s32[]{:S(2)}) async-start(), calls=%async_computation.17 | async-start | bytes 2097152 | tf_op jit(solution)/shard_map/psum | solution.py:46
  68.1 51.3 %copy-start.10 = (bf16[1,128,512]{1,2,0:T(8,128)(2,1)}, bf16[1,128,512]{1,2,0:T(8,128)(2,1)S(1)}, u32[]{:S(2)}) copy-start(bf16[1,128,512]{1,2,0:T(8,128)(2,1)S(1)} %copy.265) | copy-start | bytes 393220
  68.2 55.9 %copy-start.20 = (s32[128,8]{0,1:T(8,128)S(1)}, s32[128,8]{0,1:T(8,128)}, u32[]{:S(2)}) copy-start(s32[128,8]{0,1:T(8,128)} %param.18) | copy-start | bytes 12292
  68.4 60.3 %copy-start.29 = (f32[4,128]{1,0:T(4,128)}, f32[4,128]{1,0:T(4,128)S(1)}, u32[]{:S(2)}) copy-start(f32[4,128]{1,0:T(4,128)S(1)} %get-tuple-element.95) | copy-start | bytes 6148
  69.1 59.6 %copy-start.34 = (f32[4,128]{1,0:T(4,128)}, f32[4,128]{1,0:T(4,128)S(1)}, u32[]{:S(2)}) copy-start(f32[4,128]{1,0:T(4,128)S(1)} %fusion.61) | copy-start | bytes 6148
  69.4 59.4 %copy-start.17 = (bf16[4,128,128]{2,1,0:T(8,128)(2,1)}, bf16[4,128,128]{2,1,0:T(8,128)(2,1)S(1)}, u32[]{:S(2)}) copy-start(bf16[4,128,128]{2,1,0:T(8,128)(2,1)S(1)} %convolution_convert_fusion.5) | copy-start | bytes 393220
  115.2 59.8 %all-to-all-start.4 = ((bf16[8,16,2048]{2,1,0:T(8,128)(2,1)}), bf16[8,16,2048]{2,1,0:T(8,128)(2,1)S(1)}, u32[]{:S(2)}, u32[]{:S(2)}) async-start(bf16[8,16,2048]{2,1,0:T(8,128)(2,1)} %bitcast.30), calls=%async_computation.5 | async-start | bytes 1048576 | tf_op jit(solution)/shard_map/all_to_all | solution.py:105
  118.9 167.9 %all-gather.13.cloned.1.call-start = ((), (), s32[]{:S(2)}) async-start(), calls=%async_computation.19 | async-start | bytes 2621440 | tf_op jit(solution)/shard_map/all_gather | solution.py:116
  175.9 105.2 %all-to-all-start.1 = ((bf16[8,2,80,2048]{3,2,1,0:T(8,128)(2,1)}), bf16[8,2,80,2048]{3,2,1,0:T(8,128)(2,1)}, u32[]{:S(2)}, u32[]{:S(2)}) async-start(bf16[8,2,80,2048]{3,2,1,0:T(8,128)(2,1)} %bitcast.185), calls=%async_computation.1 | async-start | bytes 10485760 | tf_op jit(solution)/shard_map/all_to_all | solution.py:50
  180.5 112.0 %all-gather.11.cloned.1.call-start = ((), (), s32[]{:S(2)}) async-start(), calls=%async_computation.18 | async-start | bytes 2621440 | tf_op jit(solution)/shard_map/all_gather | solution.py:115
  281.0 65.6 %all-to-all-start.5 = ((bf16[8,2,80,2048]{3,2,1,0:T(8,128)(2,1)}), bf16[8,2,80,2048]{3,2,1,0:T(8,128)(2,1)}, u32[]{:S(2)}, u32[]{:S(2)}) async-start(bf16[8,2,80,2048]{3,2,1,0:T(8,128)(2,1)} %bitcast.186), calls=%async_computation.6 | async-start | bytes 10485760 | tf_op jit(solution)/shard_map/all_to_all | solution.py:50
  285.7 33.4 %all-gather.15.cloned.1.call-start = ((), (), s32[]{:S(2)}) async-start(), calls=%async_computation.20 | async-start | bytes 2621440 | tf_op jit(solution)/shard_map/all_gather | solution.py:117
  286.3 125.9 %reduce-scatter.12.cloned.1.call-start = ((), (), s32[]{:S(2)}) async-start(), calls=%async_computation.21 | async-start | bytes 6553600 | tf_op jit(solution)/shard_map/reduce_scatter | solution.py:54
  414.7 23.2 %all-to-all-start.2 = ((bf16[8,2,80,512]{3,2,1,0:T(8,128)(2,1)}), bf16[8,2,80,512]{3,2,1,0:T(8,128)(2,1)S(1)}, u32[]{:S(2)}, u32[]{:S(2)}) async-start(bf16[8,2,80,512]{3,2,1,0:T(8,128)(2,1)} %copy.221), calls=%async_computation.3 | async-start | bytes 2621440 | tf_op jit(solution)/shard_map/all_to_all | solution.py:60
  636.4 65.7 %all-to-all-start.6 = ((bf16[8,2,80,2048]{3,2,1,0:T(8,128)(2,1)}), bf16[8,2,80,2048]{3,2,1,0:T(8,128)(2,1)}, u32[]{:S(2)}, u32[]{:S(2)}) async-start(bf16[8,2,80,2048]{3,2,1,0:T(8,128)(2,1)} %copy.228), calls=%async_computation.7 | async-start | bytes 10485760 | tf_op jit(solution)/shard_map/all_to_all | solution.py:50
  641.2 147.7 %all-reduce.11.cloned.1.call-start = ((), (), s32[]{:S(2)}) async-start(), calls=%async_computation.22 | async-start | bytes 2097152 | tf_op jit(solution)/shard_map/psum | solution.py:46
  641.9 83.0 %copy-start.25 = (bf16[128,16]{0,1:T(8,128)(2,1)}, bf16[128,16]{0,1:T(8,128)(2,1)S(1)}, u32[]{:S(2)}) copy-start(bf16[128,16]{0,1:T(8,128)(2,1)S(1)} %select_reduce_fusion) | copy-start | bytes 12292
  744.3 77.7 %reduce-scatter.20.cloned.1.call-start = ((), (), s32[]{:S(2)}) async-start(), calls=%async_computation.26 | async-start | bytes 2621440 | tf_op jit(solution)/shard_map/reduce_scatter | solution.py:316
  750.9 73.3 %reduce-scatter.18.cloned.1.call-start = ((), (), s32[]{:S(2)}) async-start(), calls=%async_computation.25 | async-start | bytes 2621440 | tf_op jit(solution)/shard_map/reduce_scatter | solution.py:313
  757.4 85.5 %reduce-scatter.16.cloned.1.call-start = ((), (), s32[]{:S(2)}) async-start(), calls=%async_computation.24 | async-start | bytes 2621440 | tf_op jit(solution)/shard_map/reduce_scatter | solution.py:310
  764.2 159.3 %reduce-scatter.22.cloned.1.call-start = ((), (), s32[]{:S(2)}) async-start(), calls=%async_computation.27 | async-start | bytes 540672
  767.0 236.6 %reduce-scatter.24.cloned.1.call-start = ((), (), s32[]{:S(2)}) async-start(), calls=%async_computation.28 | async-start | bytes 540672
  793.8 333.5 %all-reduce.13.cloned.1.call-start = ((), (), s32[]{:S(2)}) async-start(), calls=%async_computation.29 | async-start | bytes 16777216
  812.7 396.5 %reduce-scatter.14.cloned.1.call-start = ((), (), s32[]{:S(2)}) async-start(), calls=%async_computation.23 | async-start | bytes 2162688 | tf_op jit(solution)/shard_map/reduce_scatter | solution.py:299
  815.6 110.8 %copy-start.40 = (f32[128]{0:T(128)S(1)}, f32[128]{0:T(128)}, u32[]{:S(2)}) copy-start(f32[128]{0:T(128)} %get-tuple-element.75) | copy-start | bytes 1540
  815.6 110.8 %copy-start.33 = (f32[128]{0:T(128)S(1)}, f32[128]{0:T(128)}, u32[]{:S(2)}) copy-start(f32[128]{0:T(128)} %copy-done.32) | copy-start | bytes 1540
  816.3 108.6 %all-to-all-start.3 = ((bf16[8,16,512]{2,1,0:T(8,128)(2,1)}), bf16[8,16,512]{2,1,0:T(8,128)(2,1)S(1)}, u32[]{:S(2)}, u32[]{:S(2)}) async-start(bf16[8,16,512]{2,1,0:T(8,128)(2,1)} %bitcast.28), calls=%async_computation.4 | async-start | bytes 262144 | tf_op jit(solution)/shard_map/all_to_all | solution.py:322
  928.2 76.7 %all-to-all-start.7 = ((bf16[8,16,512]{2,1,0:T(8,128)(2,1)}), bf16[8,16,512]{2,1,0:T(8,128)(2,1)S(1)}, u32[]{:S(2)}, u32[]{:S(2)}) async-start(bf16[8,16,512]{2,1,0:T(8,128)(2,1)} %bitcast.50), calls=%async_computation.8 | async-start | bytes 262144 | tf_op jit(solution)/shard_map/all_to_all | solution.py:329
  (35 other events, 426.6 us)
Sparse Core Ops, SparseCore 0:
  11.2 52.7 all-gather.6
  66.3 42.8 all-gather.8
  112.7 45.3 all-reduce.8
  358.5 53.6 reduce-scatter.11
  744.4 44.4 all-reduce.10
Sparse Core Ops, SparseCore 1:
  121.1 31.5 all-gather.12
  182.8 31.5 all-gather.10
  288.0 31.1 all-gather.14
  751.0 28.2 reduce-scatter.19
  781.8 29.3 reduce-scatter.17
  813.5 29.3 reduce-scatter.15
  846.5 76.9 reduce-scatter.21
  927.2 76.3 reduce-scatter.23
  1007.2 120.1 all-reduce.12
  1130.9 78.2 reduce-scatter.13
where the time goes:
time: 1230 us; the launch traced here: 1220 us
  waiting for transfers between devices  665 us (54%)
  blocking collectives  257 us (21%)
  local copies, waits for them, and re-layouts  116 us (9%)
  matrix products  79.1 us (6%)
  other arithmetic  46.3 us (4%)
  starting transfers between devices  37.1 us (3%)
  between operations  17 us (1%)
    unnamed x18, waiting for transfers between devices  274 us
    psum x1, blocking collectives, local(): grad_sent, gate_dots = lax.psum((grad_sent, gate_dot_part), 'tensor')  182 us
    all_to_all x3, waiting for transfers between devices, whole_move(): lax.all_to_all(buffer, 'expert', split_axis=0, concat_axis=0, tiled=True)  87.7 us
    reduce_scatter x1, waiting for transfers between devices, local(): lax.psum_scatter(grad_out_w.astype(jnp.bfloat16), ('dp', 'expert'), scatt...  80 us
    all_gather x1, blocking collectives, local(): lax.all_gather(router_weight, ('dp', 'expert'), axis=1, tiled=True)  74.8 us
    reduce_scatter x1, waiting for transfers between devices, share_sum(): lax.psum_scatter(terms.astype(jnp.bfloat16), 'tensor', scatter_dimension=...  52.7 us
    psum x2, waiting for transfers between devices, head_total(): return lax.psum(partial_rows, 'tensor')  41.1 us
    all_gather x1, waiting for transfers between devices, local(): lax.all_gather(out_weight, ('dp', 'expert'), axis=1, tiled=True)  39.8 us
  transfers between devices with their start and end apart: 23, of which 15 were waited for; matrix products, arithmetic and copies ran while one was open for 13% of the time, Pallas kernels for 0%

commit v1 on v0

v1 whole, which is shorter than its diff:
```python
import jax
import jax.numpy as jnp
from jax import lax
from jax.sharding import Mesh
from jax.sharding import PartitionSpec as P

HEAD_DIM = 128
EPSILON = 1e-05
F32 = jnp.float32
BF16 = jnp.bfloat16
BIG = 1 << 30


def shift(values, axis, step):
    size = lax.axis_size(axis)
    return lax.ppermute(values, axis, [(i, (i + step) % size) for i in range(size)])


def pick(parts, index):
    return lax.dynamic_index_in_dim(parts, index, 0, keepdims=False)


def ring_sum(parts, axis):
    size = lax.axis_size(axis)
    me = lax.axis_index(axis)
    total = pick(parts, me).astype(F32)
    got = [shift(pick(parts, (me + k) % size), axis, k) for k in (1, size - 1, 2)]
    for piece in got:
        total = total + piece.astype(F32)
    return total


def ring_gather(values, axis):
    size = lax.axis_size(axis)
    me = lax.axis_index(axis)
    held = {0: values}
    for k in (size - 1, 1, 2):
        held[(size - k) % size] = shift(values, axis, k)
    stacked = jnp.stack([held[k] for k in range(size)])
    return [pick(stacked, (j - me) % size) for j in range(size)]


def core_swap(values):
    return lax.ppermute(values, "core", [(0, 1), (1, 0)])


def hi_lo(values):
    high = values.astype(BF16)
    return high, (values - high.astype(F32)).astype(BF16)


def segment_of(seq_lengths, row_count):
    seq_ends = jnp.cumsum(seq_lengths)
    position = jnp.arange(row_count, dtype=jnp.int32)
    return jnp.sum((position[:, None] >= seq_ends[None, :]).astype(jnp.int32), axis=1)


def local(
    tokens,
    cotangent,
    seq_lengths,
    deal_order,
    expert_ids,
    slot_order,
    qkv_weight,
    out_weight,
    router_weight,
    gate_weight,
    up_weight,
    down_weight,
    gain_first,
    gain_second,
):
    rows, width = tokens.shape
    zc = ("z", "core")
    peers = lax.axis_size("z") * lax.axis_size("core")
    tensors = lax.axis_size("tensor")
    dps = lax.axis_size("dp")
    zs = lax.axis_size("z")
    share = rows // peers
    part = width // tensors
    me_core = lax.axis_index("core")
    me_z = lax.axis_index("z")
    me = me_z * 2 + me_core
    me_y = lax.axis_index("tensor")
    experts = router_weight.shape[0]
    top = expert_ids.shape[1]
    capacity = (5 * rows * top + 4 * experts - 1) // (4 * experts)
    here = gate_weight.shape[0]
    hidden_part = gate_weight.shape[2]
    head_width = qkv_weight.shape[2]
    heads = head_width // HEAD_DIM
    scale = HEAD_DIM ** (-0.5)
    feats = qkv_weight.shape[1]

    attn_local = jnp.concatenate(
        [
            qkv_weight[0],
            qkv_weight[1],
            qkv_weight[2],
            out_weight.T,
            jnp.pad(router_weight.T, ((0, 0), (0, 128 - experts))),
        ],
        axis=1,
    )
    attn_full = lax.all_gather(attn_local, ("dp", "z", "core"), axis=0, tiled=True)
    expert_local = jnp.concatenate([gate_weight, up_weight, down_weight], axis=0)
    expert_full = lax.all_gather(expert_local, "dp", axis=1, tiled=True)

    dest_group = deal_order // rows % peers
    place = dest_group * share + (deal_order % rows - me * share)
    deal_matrix = (place[None, :] == jnp.arange(rows, dtype=jnp.int32)[:, None]).astype(BF16)
    both = jnp.dot(
        deal_matrix, jnp.concatenate([tokens, cotangent], axis=1), preferred_element_type=F32
    ).astype(BF16)
    got = lax.all_to_all(
        both[:, :width].reshape(peers, share, width), zc, split_axis=0, concat_axis=0, tiled=True
    )
    resid_in = got.reshape(rows, width).astype(F32)
    cot_part = lax.dynamic_slice_in_dim(both[:, width:], me_y * part, part, 1)
    cot_cols = lax.all_gather(cot_part, zc, axis=0, tiled=False)
    cot_cols = cot_cols.reshape(peers, peers, share, part).transpose(1, 0, 2, 3)
    cot_all = lax.all_gather(
        cot_cols.reshape(peers * rows, part), "tensor", axis=1, tiled=True
    )
    cot_all3 = cot_all.reshape(peers, rows, width)
    upstream = lax.dynamic_index_in_dim(cot_all3, me, 0, keepdims=False).astype(F32)

    match = expert_ids[:, :, None] == jnp.arange(experts, dtype=jnp.int32)[None, None, :]
    order = jnp.min(jnp.where(match, slot_order[:, :, None], BIG), axis=1)
    chosen = order < BIG
    earlier = jnp.sum((order[None, :, :] < order[:, None, :]).astype(jnp.int32), axis=1)
    code = chosen.astype(F32) + (chosen & (earlier < capacity)).astype(F32)
    code_all = lax.all_gather(
        jnp.pad(code, ((0, 0), (0, 128 - experts))).astype(BF16), zc, axis=0, tiled=True
    )[:, :experts]
    chosen_all = code_all > 0.5
    kept_all = code_all > 1.5

    factor_first = lax.rsqrt(jnp.mean(resid_in * resid_in, axis=-1, keepdims=True) + EPSILON)
    unit_first = resid_in * factor_first
    normed = (unit_first * gain_first).astype(BF16)
    qkv_full = attn_full[:, : 3 * head_width]
    out_t = attn_full[:, 3 * head_width : 4 * head_width]
    router_t = attn_full[:, 4 * head_width : 4 * head_width + experts]
    projected = jnp.dot(normed, qkv_full, preferred_element_type=F32).astype(BF16)
    queries = projected[:, :head_width].reshape(rows, heads, HEAD_DIM)
    keys = projected[:, head_width : 2 * head_width].reshape(rows, heads, HEAD_DIM)
    values = projected[:, 2 * head_width :].reshape(rows, heads, HEAD_DIM)
    segment = segment_of(seq_lengths[0], rows)
    same_seq = (segment[:, None] == segment[None, :])[None, :, :]
    scores = jnp.einsum("qhd,khd->hqk", queries, keys, preferred_element_type=F32) * scale
    scores = jnp.where(same_seq, scores, -1000000000.0)
    peak = jnp.max(scores, axis=-1, keepdims=True)
    exponent = jnp.exp(scores - peak)
    weights = exponent / jnp.sum(exponent, axis=-1, keepdims=True)
    weights_low = weights.astype(BF16)
    mixed = jnp.einsum("hqk,khd->qhd", weights_low, values, preferred_element_type=F32)
    mixed = mixed.astype(BF16).reshape(rows, head_width)
    mixed_all = lax.all_gather(mixed, zc, axis=0, tiled=True)
    branch = lax.dot_general(
        mixed, out_t, (((1,), (1,)), ((), ())), preferred_element_type=F32
    ).astype(BF16)
    branch = branch.reshape(rows, tensors, part).transpose(1, 0, 2)
    resid_part = lax.dynamic_slice_in_dim(resid_in, me_y * part, part, 1) + ring_sum(
        branch, "tensor"
    )
    resid_rows = jnp.concatenate(ring_gather(resid_part.astype(BF16), "tensor"), axis=1)
    resid_z = jnp.stack(ring_gather(resid_rows, "z"))
    resid_other = core_swap(resid_z)
    first = jnp.where(me_core == 0, resid_z, resid_other)
    second = jnp.where(me_core == 0, resid_other, resid_z)
    resid_all = jnp.stack([first, second], axis=1).reshape(peers * rows, width).astype(F32)

    factor_all = lax.rsqrt(jnp.mean(resid_all * resid_all, axis=-1, keepdims=True) + EPSILON)
    hidden = (resid_all * factor_all * gain_second).astype(BF16)
    logits = jnp.dot(hidden, router_t, preferred_element_type=F32)
    top_logit = jnp.max(jnp.where(chosen_all, logits, -jnp.inf), axis=-1, keepdims=True)
    lifted = jnp.where(chosen_all, jnp.exp(logits - top_logit), 0.0)
    gates_all = lifted / jnp.sum(lifted, axis=-1, keepdims=True)
    used_all = jnp.where(kept_all, gates_all, 0.0)
    used = lax.dynamic_slice_in_dim(used_all, me * here, here, 1)
    gate_w = expert_full[:here]
    up_w = expert_full[here : 2 * here]
    down_w = expert_full[2 * here :]
    gate_part = jnp.einsum("td,edf->tef", hidden, gate_w, preferred_element_type=F32)
    up_part = jnp.einsum("td,edf->tef", hidden, up_w, preferred_element_type=F32)
    sigmoid = jax.nn.sigmoid(gate_part)
    silu = gate_part * sigmoid
    active = silu * up_part
    active_used = (active * used[:, :, None]).astype(BF16)
    back = jnp.einsum("td,edf->tef", cot_all, down_w, preferred_element_type=F32)
    gate_dot = jnp.sum(back * active, axis=-1)
    back = back * used[:, :, None]
    grad_gate = (back * up_part * sigmoid * (1.0 + gate_part * (1.0 - sigmoid))).astype(BF16)
    grad_up = (back * silu).astype(BF16)
    grad_rows = jnp.einsum("tef,edf->td", grad_gate, gate_w, preferred_element_type=F32)
    grad_rows = grad_rows + jnp.einsum("tef,edf->td", grad_up, up_w, preferred_element_type=F32)
    kept_here = lax.dynamic_slice_in_dim(kept_all, me * here, here, 1)
    gate_dot = jnp.where(kept_here, gate_dot, 0.0)
    dot_table = jnp.zeros((peers * rows, experts), F32)
    dot_table = lax.dynamic_update_slice_in_dim(dot_table, gate_dot, me * here, 1)
    dot_high, dot_low = hi_lo(dot_table)
    dot_cols = jnp.concatenate(
        [dot_high, dot_low, jnp.zeros((peers * rows, 128 - 2 * experts), BF16)], axis=1
    )
    sent = jnp.concatenate([grad_rows.astype(BF16), dot_cols], axis=1)
    sent = sent.reshape(zs, 2, rows, width + 128)
    own = lax.dynamic_index_in_dim(sent, me_core, 1, keepdims=False)
    swapped = core_swap(lax.dynamic_index_in_dim(sent, 1 - me_core, 1, keepdims=False))
    paired = (own.astype(F32) + swapped.astype(F32)).astype(BF16)
    at_group = ring_sum(paired, "z")
    dots_here = at_group[:, width : width + experts] + at_group[:, width + experts : width + 2 * experts]
    dots_here = jnp.concatenate(
        [*hi_lo(dots_here), jnp.zeros((rows, 128 - 2 * experts), BF16)], axis=1
    )
    cols = at_group[:, :width].astype(BF16).reshape(rows, tensors, part).transpose(1, 0, 2)
    cols = jnp.concatenate(
        [cols, jnp.broadcast_to(dots_here[None], (tensors, rows, 128))], axis=2
    )
    cols = ring_sum(cols, "tensor")
    dots = cols[:, part : part + experts] + cols[:, part + experts : part + 2 * experts]
    grad_hidden = jnp.concatenate(ring_gather(cols[:, :part].astype(BF16), "tensor"), axis=1).astype(F32)

    def own_rows(table):
        return lax.dynamic_slice_in_dim(table, me * rows, rows, 0)

    gates = own_rows(gates_all)
    hidden_here = own_rows(hidden)
    grad_logits = (gates * (dots - jnp.sum(dots * gates, axis=-1, keepdims=True))).astype(BF16)
    grad_hidden = grad_hidden + lax.dot_general(
        grad_logits, router_t, (((1,), (1,)), ((), ())), preferred_element_type=F32
    )
    grad_router = lax.dot_general(
        grad_logits, hidden_here, (((0,), (0,)), ((), ())), preferred_element_type=F32
    )
    factor_second = own_rows(factor_all)
    unit_second = own_rows(resid_all) * factor_second
    grad_gain_second = jnp.sum(grad_hidden * unit_second, axis=0)
    scaled = grad_hidden * gain_second
    grad_resid = upstream + factor_second * (
        scaled - unit_second * jnp.mean(scaled * unit_second, axis=-1, keepdims=True)
    )
    grad_branch = grad_resid.astype(BF16)

    grad_mixed = jnp.dot(grad_branch, out_t, preferred_element_type=F32)
    grad_mixed = grad_mixed.astype(BF16).reshape(rows, heads, HEAD_DIM)
    grad_values = jnp.einsum(
        "hqk,qhd->khd", weights_low, grad_mixed, preferred_element_type=F32
    ).astype(BF16)
    grad_weights = jnp.einsum("qhd,khd->hqk", grad_mixed, values, preferred_element_type=F32)
    offset = jnp.sum(grad_weights * weights, axis=-1, keepdims=True)
    grad_scores = (weights * (grad_weights - offset)).astype(BF16)
    grad_queries = (
        jnp.einsum("hqk,khd->qhd", grad_scores, keys, preferred_element_type=F32) * scale
    ).astype(BF16)
    grad_keys = (
        jnp.einsum("hqk,qhd->khd", grad_scores, queries, preferred_element_type=F32) * scale
    ).astype(BF16)
    grad_proj = jnp.concatenate(
        [
            grad_queries.reshape(rows, head_width),
            grad_keys.reshape(rows, head_width),
            grad_values.reshape(rows, head_width),
        ],
        axis=1,
    )
    grad_proj_all = lax.all_gather(grad_proj, zc, axis=0, tiled=True)

    def by_feature(table):
        count = table.shape[0]
        return (
            table.reshape(count, dps, peers, feats)
            .transpose(2, 0, 1, 3)
            .reshape(peers, count, dps * feats)
        )

    def to_feature(table):
        return lax.all_to_all(by_feature(table), zc, split_axis=0, concat_axis=0, tiled=True)

    normed_feat = to_feature(normed).reshape(peers * rows, dps * feats)
    branch_feat = to_feature(grad_branch).reshape(peers * rows, dps * feats)
    grad_out_t = lax.dot_general(
        branch_feat, mixed_all, (((0,), (0,)), ((), ())), preferred_element_type=F32
    )

    grad_normed = lax.dot_general(
        grad_proj, qkv_full, (((1,), (1,)), ((), ())), preferred_element_type=F32
    )
    gain_unit = gain_first * unit_first
    inner = jnp.sum(grad_normed * gain_unit, axis=-1, keepdims=True)
    grad_gain_first = jnp.sum(grad_normed * unit_first, axis=0)
    inner_cols = jnp.concatenate([*hi_lo(inner), jnp.zeros((rows, 126), BF16)], axis=1)
    normed_cols = grad_normed.astype(BF16).reshape(rows, tensors, part).transpose(1, 0, 2)
    normed_cols = jnp.concatenate(
        [normed_cols, jnp.broadcast_to(inner_cols[None], (tensors, rows, 128))], axis=2
    )
    normed_cols = ring_sum(normed_cols, "tensor")
    inner = (normed_cols[:, part : part + 1] + normed_cols[:, part + 1 : part + 2]) / width

    def own_cols(table):
        return lax.dynamic_slice_in_dim(table, me_y * part, part, table.ndim - 1)

    input_part = own_cols(grad_resid) + factor_first * (
        normed_cols[:, :part] * own_cols(gain_first) - own_cols(unit_first) * inner
    )

    gain_first_sum = sum(
        piece for piece in ring_gather(grad_gain_first.reshape(16, -1), "tensor")
    ).reshape(1, width)
    small = jnp.concatenate(
        [
            grad_router,
            grad_gain_second[None],
            gain_first_sum,
            jnp.zeros((32 - experts - 2, width), F32),
        ],
        axis=0,
    ).astype(BF16)
    small = jnp.sum(to_feature(small).astype(F32), axis=0)

    grad_qkv = lax.dot_general(
        normed_feat, grad_proj_all, (((0,), (0,)), ((), ())), preferred_element_type=F32
    )
    by_dp = jnp.concatenate(
        [
            grad_qkv.astype(BF16),
            grad_out_t.astype(BF16),
            jnp.pad(small.T, ((0, 0), (0, 96))).astype(BF16),
        ],
        axis=1,
    ).reshape(dps, feats, 4 * head_width + 128)
    by_dp = ring_sum(by_dp, "dp")
    qkv_grad = by_dp[:, : 3 * head_width].reshape(feats, 3, head_width).transpose(1, 0, 2)
    out_grad = by_dp[:, 3 * head_width : 4 * head_width].T
    tail = by_dp[:, 4 * head_width :]
    router_grad = tail[:, :experts].T
    gain_second_grad = tail[:, experts]
    gain_first_grad = tail[:, experts + 1]

    grad_gate_w = jnp.einsum("td,tef->edf", hidden, grad_gate, preferred_element_type=F32)
    grad_up_w = jnp.einsum("td,tef->edf", hidden, grad_up, preferred_element_type=F32)
    grad_down = jnp.einsum("td,tef->edf", cot_all, active_used, preferred_element_type=F32)
    expert_grads = jnp.concatenate(
        [g.astype(BF16).reshape(here, dps, -1, hidden_part) for g in (grad_gate_w, grad_up_w, grad_down)],
        axis=0,
    ).transpose(1, 0, 2, 3)
    expert_grads = lax.psum_scatter(expert_grads, "dp", scatter_dimension=0, tiled=False).astype(F32)

    expert_rows = jnp.einsum("tef,edf->td", active_used, down_w, preferred_element_type=F32)
    expert_rows = lax.psum_scatter(
        expert_rows.astype(BF16).reshape(peers, rows, width), zc, scatter_dimension=0, tiled=False
    )
    expert_rows = lax.psum_scatter(
        expert_rows.reshape(rows, tensors, part).transpose(1, 0, 2),
        "tensor",
        scatter_dimension=0,
        tiled=False,
    ).astype(F32)
    output_part = resid_part + expert_rows

    final = jnp.concatenate([output_part.astype(BF16), input_part.astype(BF16)], axis=1)
    final = lax.all_to_all(
        final.reshape(peers, share, 2 * part), zc, split_axis=0, concat_axis=0, tiled=True
    ).reshape(rows, 2 * part)
    final = lax.dot_general(
        deal_matrix, final, (((0,), (0,)), ((), ())), preferred_element_type=F32
    ).astype(BF16)
    return (
        final[:, :part],
        final[:, part:],
        qkv_grad,
        out_grad,
        router_grad,
        expert_grads[:here],
        expert_grads[here : 2 * here],
        expert_grads[2 * here :],
        gain_first_grad,
        gain_second_grad,
    )


def solution(mesh):
    sizes = mesh.shape
    split = Mesh(
        mesh.devices.reshape(sizes["dp"], sizes["expert"] // 2, 2, sizes["tensor"]),
        ("dp", "z", "core", "tensor"),
    )
    experts = ("z", "core")
    every = ("dp", "z", "core")
    placed = (
        P(every, None),
        P(every, None),
        P(every, None),
        P(every),
        P(every, None),
        P(every, None),
        P(None, every, "tensor"),
        P("tensor", every),
        P(None, every),
        P(experts, "dp", "tensor"),
        P(experts, "dp", "tensor"),
        P(experts, "dp", "tensor"),
        P(),
        P(),
    )
    return jax.shard_map(
        local,
        mesh=split,
        in_specs=placed,
        out_specs=(
            P(every, "tensor"),
            P(every, "tensor"),
            P(None, every, "tensor"),
            P("tensor", every),
            P(None, every),
            P(experts, "dp", "tensor"),
            P(experts, "dp", "tensor"),
            P(experts, "dp", "tensor"),
            P(every),
            P(every),
        ),
        check_vma=False,
    )
```

time: 1230 us -> 517 us (0.42)
  waiting for transfers between devices: 665 us -> 204 us
  blocking collectives: 257 us -> 11.7 us
  starting transfers between devices: 37.1 us -> 77.6 us
  local copies, waits for them, and re-layouts: 116 us -> 78 us
    unnamed x18 -> x9, waiting for transfers between devices: 274 us -> 0.15 us
    psum x1 -> x0, blocking collectives: 182 us -> none  [local(): grad_sent, gate_dots = lax.psum((grad_sent, gate_dot_part), 'tensor')]
    reduce_scatter x5 -> x3, waiting for transfers between devices: 149 us -> 0.02 us  [the longest x1 0.02 us: local(): lax.psum_scatter(expert_rows.astype(BF16).reshape(peers, rows, width), zc...]
    ppermute x0 -> x29, waiting for transfers between devices: none -> 99 us  [the longest x27 96.7 us: shift(): lax.ppermute(values, axis, [(i, (i + step) % size) for i in range(size)])]
    all_to_all x8 -> x5, waiting for transfers between devices: 108 us -> 26 us  [the longest x1 13.1 us: local(): lax.all_to_all(both[:, :width].reshape(peers, share, width), zc, split_ax...]
    all_gather x1, blocking collectives: 74.8 us -> 11.7 us  [local(): lax.all_gather(jnp.pad(code, ((0, 0), (0, 128 - experts))).astype(BF16),...]
    ppermute x0 -> x29, starting transfers between devices: none -> 43.6 us  [the longest x27 43.6 us: shift(): lax.ppermute(values, axis, [(i, (i + step) % size) for i in range(size)])]
    psum x2 -> x0, waiting for transfers between devices: 41.1 us -> none  [head_total(): return lax.psum(partial_rows, 'tensor')]
  transfers between devices with their start and end apart: 23 -> 43, of which waited for: 15 -> 28; matrix products, arithmetic and copies ran while one was open for 13% -> 33% of each run, Pallas kernels for 0% -> 0%
where the time goes in v1:
time: 517 us; the launch traced here: 507 us
  waiting for transfers between devices  204 us (39%)
  matrix products  85.2 us (16%)
  local copies, waits for them, and re-layouts  78 us (15%)
  starting transfers between devices  77.6 us (15%)
  other arithmetic  35.2 us (7%)
  between operations  15.5 us (3%)
  blocking collectives  11.7 us (2%)
    ppermute x27, waiting for transfers between devices, shift(): lax.ppermute(values, axis, [(i, (i + step) % size) for i in range(size)])  96.7 us
    ppermute x27, starting transfers between devices, shift(): lax.ppermute(values, axis, [(i, (i + step) % size) for i in range(size)])  43.6 us
    all_gather x1, waiting for transfers between devices, local(): lax.all_gather(cot_cols.reshape(peers * rows, part), 'tensor', axis=1, ti...  39.1 us
    all_gather x1, waiting for transfers between devices, local(): lax.all_gather(attn_local, ('dp', 'z', 'core'), axis=0, tiled=True)  33 us
    reshape x6, local copies, waits for them, and re-layouts, local(): g.astype(BF16).reshape(here, dps, -1, hidden_part)  18.3 us
    unnamed x92, local copies, waits for them, and re-layouts  13.2 us
    all_to_all x1, waiting for transfers between devices, local(): lax.all_to_all(both[:, :width].reshape(peers, share, width), zc, split_ax...  13.1 us
    all_to_all x3, starting transfers between devices, to_feature(): lax.all_to_all(by_feature(table), zc, split_axis=0, concat_axis=0, tiled=...  12.6 us
  transfers between devices with their start and end apart: 43, of which 28 were waited for; matrix products, arithmetic and copies ran while one was open for 33% of the time, Pallas kernels for 0%

profile of v1, /device:TPU:0, one launch (start us, length us, event | category | flops | bytes accessed | tf_op | source)
XLA Modules:
  0.0 506.8 jit_solution(5080080587751398570)
XLA Ops:
  18.8 5.4 %all-to-all-start = ((bf16[8,16,2048]{2,1,0:T(8,128)(2,1)}), bf16[8,16,2048]{2,1,0:T(8,128)(2,1)S(1)}, u32[]{:S(2)}, u32[]{:S(2)}) async-start(bf16[8,16,2048]{2,1,0:T(8,128)(2,1)} %bitcast), calls=%async_computation | async-start | bytes 1048576 | tf_op jit(solution)/shard_map/all_to_all | solution.py:116
  24.6 13.1 %all-to-all-done = bf16[8,16,2048]{2,1,0:T(8,128)(2,1)S(1)} async-done(((bf16[8,16,2048]{2,1,0:T(8,128)(2,1)}), bf16[8,16,2048]{2,1,0:T(8,128)(2,1)S(1)}, u32[]{:S(2)}, u32[]{:S(2)}) %all-to-all-start) | async-done | bytes 524320 | tf_op jit(solution)/shard_map/all_to_all | solution.py:116
  39.2 33.0 %all-gather.8.cloned.1.call-done = bf16[2048,2176]{1,0:T(8,128)(2,1)} async-done(((bf16[64,2176]{1,0:T(8,128)(2,1)}), bf16[2048,2176]{1,0:T(8,128)(2,1)}) %all-gather.8.cloned.1.call-update) | async-done | bytes 8912912 | tf_op jit(solution)/shard_map/all_gather | solution.py:106
  108.9 10.5 %collective-permute-done.8 = bf16[128,2048]{1,0:T(8,128)(2,1)S(1)} collective-permute-done((bf16[128,2048]{1,0:T(8,128)(2,1)S(1)}, bf16[128,2048]{1,0:T(8,128)(2,1)S(1)}, u32[]{:S(2)}, u32[]{:S(2)}) %collective-permute-start.8) | collective-permute-done | bytes 524320 | tf_op jit(solution)/shard_map/ppermute | solution.py:16
  119.4 10.3 %collective-permute-done.7 = bf16[128,2048]{1,0:T(8,128)(2,1)S(1)} collective-permute-done((bf16[128,2048]{1,0:T(8,128)(2,1)S(1)}, bf16[128,2048]{1,0:T(8,128)(2,1)S(1)}, u32[]{:S(2)}, u32[]{:S(2)}) %collective-permute-start.7) | collective-permute-done | bytes 524320 | tf_op jit(solution)/shard_map/ppermute | solution.py:16
  137.3 11.7 %all_gather.26 = bf16[1024,128]{0,1:T(8,128)(2,1)S(1)} all-gather(bf16[128,128]{0,1:T(8,128)(2,1)S(1)} %pad.15), channel_id=1, replica_groups=mesh['dp'=4,'z'=4,'core'=2,'tensor'=4] {'z','core'}, dimensions={0}, use_global_device_ids=true | all-gather | bytes 294912 | tf_op jit(solution)/shard_map/all_gather | solution.py:134
  158.6 6.2 %all-gather.10.cloned.1.call-done = bf16[6,2048,256]{1,2,0:T(8,128)(2,1)} async-done(((bf16[6,512,256]{1,2,0:T(8,128)(2,1)}), bf16[6,2048,256]{1,2,0:T(8,128)(2,1)}) %all-gather.10.cloned.1.call-update) | async-done | bytes 6291472 | tf_op jit(solution)/shard_map/all_gather | solution.py:108
  164.8 6.7 %fusion.15 = f32[1024,2,256]{0,2,1:T(8,128)} fusion(bf16[1024,2048]{1,0:T(8,128)(2,1)} %copy-done.1, bf16[6,2048,256]{1,2,0:T(8,128)(2,1)} %all-gather.10.cloned.1.call-done), kind=kOutput, calls=%fused_computation.23 | convolution fusion | flops 2147483648 | bytes 8388608 | tf_op jit(solution)/shard_map/td,edf->tef/dot_general | solution.py:187
  171.5 5.3 %fusion.17 = f32[1024,2,256]{0,2,1:T(8,128)} fusion(bf16[1024,2048]{1,0:T(8,128)(2,1)S(1)} %copy-done.2, bf16[6,2048,256]{1,2,0:T(8,128)(2,1)} %all-gather.10.cloned.1.call-done), kind=kOutput, calls=%fused_computation.25 | convolution fusion | flops 2147483648 | bytes 8388608 | tf_op jit(solution)/shard_map/td,edf->tef/dot_general | solution.py:186
  176.8 39.1 %all-gather.12.cloned.1.call-done = bf16[1024,2048]{1,0:T(8,128)(2,1)} async-done(((bf16[1024,512]{1,0:T(8,128)(2,1)}), bf16[1024,2048]{1,0:T(8,128)(2,1)}) %all-gather.12.cloned.1.call-update) | async-done | bytes 4194320 | tf_op jit(solution)/shard_map/all_gather | solution.py:123
  215.9 8.3 %multiply_reduce_fusion.1 = (f32[1024,2]{0,1:T(2,128)S(1)}, bf16[1024,2,256]{0,2,1:T(8,128)(2,1)S(1)}, bf16[1024,2,256]{0,2,1:T(8,128)(2,1)S(1)}, bf16[1024,2,256]{0,2,1:T(8,128)(2,1)}) fusion(f32[1024,2,256]{0,2,1:T(8,128)} %fusion.15, f32[1024,2,256]{0,2,1:T(8,128)} %fusion.17, f32[1024,2]{0,1:T(2,128)S(1)} %fusion.118, ...), kind=kOutput, calls=%fused_computation.43 | convolution fusion | flops 2157443072 | bytes 13647872 | tf_op jit(solution)/shard_map/td,edf->tef/dot_general | solution.py:192
  224.2 6.7 %bitcast_convert_fusion = bf16[1024,2048]{1,0:T(8,128)(2,1)} fusion(bf16[1024,2,256]{0,2,1:T(8,128)(2,1)S(1)} %get-tuple-element.90, bf16[6,2048,256]{1,2,0:T(8,128)(2,1)} %all-gather.10.cloned.1.call-done), kind=kOutput, calls=%fused_computation.3 | convolution fusion | flops 2149580800 | bytes 7340032 | tf_op jit(solution)/shard_map/tef,edf->td/dot_general | solution.py:350
  230.9 6.5 %copy.354 = bf16[8,128,2048]{1,2,0:T(8,128)(2,1)} copy(bf16[8,128,2048]{2,1,0:T(8,128)(2,1)} %bitcast.276) | data formatting | bytes 8388608 | tf_op jit(solution)/shard_map/reshape | solution.py:352
  237.4 10.7 %all-gather.16.cloned.1.call-start = ((), (), s32[]{:S(2)}) async-start(), calls=%async_computation.14 | async-start | bytes 1179648 | tf_op jit(solution)/shard_map/all_gather | solution.py:160
  252.7 6.3 %fusion.1 = bf16[1024,2048]{1,0:T(8,128)(2,1)} fusion(f32[1024,2048,1]{1,0,2:T(8,128)S(1)} %fusion.46, bf16[1024,2,256]{0,2,1:T(8,128)(2,1)S(1)} %copy-done.36, bf16[6,2048,256]{1,2,0:T(8,128)(2,1)} %all-gather.10.cloned.1.call-done), kind=kOutput, calls=%fused_computation.2 | convolution fusion | flops 2151677952 | bytes 15728640 | tf_op jit(solution)/shard_map/tef,edf->td/dot_general | solution.py:198
  259.0 7.8 %concatenate.55 = bf16[1024,2176]{1,0:T(8,128)(2,1)} concatenate(bf16[1024,2048]{1,0:T(8,128)(2,1)} %fusion.1, bf16[1024,16]{1,0:T(8,128)(2,1)S(1)} %copy.362, bf16[1024,16]{1,0:T(8,128)(2,1)S(1)} %copy.363, bf16[1024,96]{1,0:T(8,128)(2,1)S(1)} %broadcast_in_dim.55), dimensions={1} | concatenate | bytes 8912896 | tf_op jit(solution)/shard_map/concatenate | solution.py:207
  289.2 12.0 %collective-permute-done.13 = bf16[128,2176]{0,1:T(8,128)(2,1)} collective-permute-done((bf16[128,2176]{0,1:T(8,128)(2,1)}, bf16[128,2176]{0,1:T(8,128)(2,1)}, u32[]{:S(2)}, u32[]{:S(2)}) %collective-permute-start.13) | collective-permute-done | bytes 557088 | tf_op jit(solution)/shard_map/ppermute | solution.py:16
  301.3 11.4 %collective-permute-done.12 = bf16[128,2176]{0,1:T(8,128)(2,1)} collective-permute-done((bf16[128,2176]{0,1:T(8,128)(2,1)}, bf16[128,2176]{0,1:T(8,128)(2,1)}, u32[]{:S(2)}, u32[]{:S(2)}) %collective-permute-start.12) | collective-permute-done | bytes 557088 | tf_op jit(solution)/shard_map/ppermute | solution.py:16
  318.9 4.4 collective-permute-done.16
  347.2 5.8 %fusion.31 = bf16[2,2048,256]{1,2,0:T(8,128)(2,1)} fusion(bf16[1024,2,256]{0,2,1:T(8,128)(2,1)S(1)} %copy-done.37, bf16[1024,2048]{1,0:T(8,128)(2,1)} %copy-done.1), kind=kOutput, calls=%fused_computation.31 | convolution fusion | flops 2148532224 | bytes 7340032 | tf_op jit(solution)/shard_map/td,tef->edf/dot_general | solution.py:342
  355.4 6.4 %fusion.28 = bf16[2,2048,256]{1,2,0:T(8,128)(2,1)} fusion(bf16[1024,2,256]{0,2,1:T(8,128)(2,1)} %copy-done.38, bf16[1024,2048]{1,0:T(8,128)(2,1)} %all-gather.12.cloned.1.call-done), kind=kOutput, calls=%fused_computation.30 | convolution fusion | flops 2148532224 | bytes 7340032 | tf_op jit(solution)/shard_map/td,tef->edf/dot_general | solution.py:343
  374.0 6.2 %fusion.34 = bf16[2,2048,256]{1,2,0:T(8,128)(2,1)} fusion(bf16[1024,2,256]{0,2,1:T(8,128)(2,1)} %copy-done.35, bf16[1024,2048]{1,0:T(8,128)(2,1)} %copy-done.1), kind=kOutput, calls=%fused_computation.32 | convolution fusion | flops 2148532224 | bytes 7340032 | tf_op jit(solution)/shard_map/td,tef->edf/dot_general | solution.py:341
  386.3 6.4 %maximum_bitcast_fusion = bf16[4,6,512,256]{3,2,1,0:T(8,128)(2,1)} fusion(bf16[2,4,512,256]{3,2,0,1:T(8,128)(2,1)} %copy.397, bf16[2,4,512,256]{3,2,0,1:T(8,128)(2,1)} %copy.396, bf16[2,4,512,256]{3,2,0,1:T(8,128)(2,1)} %copy.395), kind=kLoop, calls=%fused_computation.6 | loop fusion | flops 6291456 | bytes 12582912 | tf_op jit(solution)/shard_map/transpose | solution.py:347
  398.4 4.3 all-to-all-start.2
  404.3 5.4 %multiply_reduce_fusion.2 = (f32[2048]{0:T(1024)S(1)}, f32[128]{0:T(128)S(1)}, bf16[128,2048]{1,0:T(8,128)(2,1)S(1)}) fusion(f32[128,2048]{1,0:T(8,128)S(1)} %copy-done.5, f32[2048]{0:T(1024)S(1)} %copy-done.22, bf16[2048,2176]{1,0:T(8,128)(2,1)} %all-gather.8.cloned.1.call-done, bf16[128,512]{0,1:T(8,128)(2,1)} %bitcast.314, ...), kind=kOutput, calls=%fused_computation.98 | convolution fusion | flops 808056704 | bytes 8274432 | tf_op jit(solution)/shard_map/dot_general | solution.py:287
  419.0 4.8 all-to-all-start.4
  423.9 6.0 %all-to-all-done.4 = bf16[8,32,256]{2,1,0:T(8,128)(2,1)S(1)} async-done(((bf16[8,32,256]{2,1,0:T(8,128)(2,1)}), bf16[8,32,256]{2,1,0:T(8,128)(2,1)S(1)}, u32[]{:S(2)}, u32[]{:S(2)}) %all-to-all-start.4) | async-done | bytes 131104 | tf_op jit(solution)/shard_map/all_to_all | solution.py:279
  437.3 4.8 collective-permute-done.22
  456.8 10.6 %collective-permute-done.28 = bf16[64,2176]{1,0:T(8,128)(2,1)S(1)} collective-permute-done((bf16[64,2176]{1,0:T(8,128)(2,1)S(1)}, bf16[64,2176]{1,0:T(8,128)(2,1)S(1)}, u32[]{:S(2)}, u32[]{:S(2)}) %collective-permute-start.28) | collective-permute-done | bytes 278560 | tf_op jit(solution)/shard_map/ppermute | solution.py:16
  467.4 11.7 %collective-permute-done.27 = bf16[64,2176]{1,0:T(8,128)(2,1)S(1)} collective-permute-done((bf16[64,2176]{1,0:T(8,128)(2,1)S(1)}, bf16[64,2176]{1,0:T(8,128)(2,1)S(1)}, u32[]{:S(2)}, u32[]{:S(2)}) %collective-permute-start.27) | collective-permute-done | bytes 278560 | tf_op jit(solution)/shard_map/ppermute | solution.py:16
  483.5 4.4 all-to-all-start.1
  488.5 6.9 %all-to-all-done.1 = bf16[8,16,1024]{2,1,0:T(8,128)(2,1)S(1)} async-done(((bf16[8,16,1024]{2,1,0:T(8,128)(2,1)}), bf16[8,16,1024]{2,1,0:T(8,128)(2,1)S(1)}, u32[]{:S(2)}, u32[]{:S(2)}) %all-to-all-start.1) | async-done | bytes 262176 | tf_op jit(solution)/shard_map/all_to_all | solution.py:363
  (321 shorter events, 192.1 us)
Async XLA Ops:
  7.2 65.0 %all-gather.8.cloned.1.call-start = ((), (), s32[]{:S(2)}) async-start(), calls=%async_computation.8 | async-start | bytes 9191424 | tf_op jit(solution)/shard_map/all_gather | solution.py:106
  12.1 119.8 %all-gather.18.cloned.1.call-start = ((), (), s32[]{:S(2)}) async-start(), calls=%async_computation.16 | async-start | bytes 1179648 | tf_op jit(solution)/shard_map/all_gather | solution.py:121
  16.7 148.1 %all-gather.10.cloned.1.call-start = ((), (), s32[]{:S(2)}) async-start(), calls=%async_computation.9 | async-start | bytes 7864320 | tf_op jit(solution)/shard_map/all_gather | solution.py:108
  18.8 19.0 %all-to-all-start = ((bf16[8,16,2048]{2,1,0:T(8,128)(2,1)}), bf16[8,16,2048]{2,1,0:T(8,128)(2,1)S(1)}, u32[]{:S(2)}, u32[]{:S(2)}) async-start(bf16[8,16,2048]{2,1,0:T(8,128)(2,1)} %bitcast), calls=%async_computation | async-start | bytes 1048576 | tf_op jit(solution)/shard_map/all_to_all | solution.py:116
  24.2 191.7 %all-gather.12.cloned.1.call-start = ((), (), s32[]{:S(2)}) async-start(), calls=%async_computation.12 | async-start | bytes 5242880 | tf_op jit(solution)/shard_map/all_gather | solution.py:123
  81.9 7.9 %collective-permute-start.2 = (bf16[128,512]{1,0:T(8,128)(2,1)S(1)}, bf16[128,512]{1,0:T(8,128)(2,1)S(1)}, u32[]{:S(2)}, u32[]{:S(2)}) collective-permute-start(bf16[128,512]{1,0:T(8,128)(2,1)S(1)} %bitcast.302), channel_id=1, source_target_pairs={{0,2},{1,3},{2,0},{3,1},{4,6},{5,7},{6,4},{7,5},{8,10},{9,11},{10,... | collective-permute-start | bytes 393224 | tf_op jit(solution)/shard_map/ppermute | solution.py:16
  94.3 9.0 %collective-permute-start.4 = (bf16[128,512]{1,0:T(8,128)(2,1)S(1)}, bf16[128,512]{1,0:T(8,128)(2,1)S(1)}, u32[]{:S(2)}, u32[]{:S(2)}) collective-permute-start(bf16[128,512]{1,0:T(8,128)(2,1)S(1)} %get-tuple-element.82), channel_id=1, source_target_pairs={{0,2},{1,3},{2,0},{3,1},{4,6},{5,7},{6,4},{7,5},{8,10},{9,11},{10,... | collective-permute-start | bytes 393224 | tf_op jit(solution)/shard_map/ppermute | solution.py:16
  103.6 15.8 %collective-permute-start.8 = (bf16[128,2048]{1,0:T(8,128)(2,1)S(1)}, bf16[128,2048]{1,0:T(8,128)(2,1)S(1)}, u32[]{:S(2)}, u32[]{:S(2)}) collective-permute-start(bf16[128,2048]{1,0:T(8,128)(2,1)S(1)} %get-tuple-element.121), channel_id=1, source_target_pairs={{0,8},{8,16},{16,24},{24,0},{1,9},{9,17},{17,25},{25,1},{2,10},{10... | collective-permute-start | bytes 1572872 | tf_op jit(solution)/shard_map/ppermute | solution.py:16
  104.7 25.0 %collective-permute-start.7 = (bf16[128,2048]{1,0:T(8,128)(2,1)S(1)}, bf16[128,2048]{1,0:T(8,128)(2,1)S(1)}, u32[]{:S(2)}, u32[]{:S(2)}) collective-permute-start(bf16[128,2048]{1,0:T(8,128)(2,1)S(1)} %get-tuple-element.121), channel_id=1, source_target_pairs={{0,16},{8,24},{16,0},{24,8},{1,17},{9,25},{17,1},{25,9},{2,18},{10... | collective-permute-start | bytes 1572872 | tf_op jit(solution)/shard_map/ppermute | solution.py:16
  107.5 22.3 %collective-permute-start.6 = (bf16[128,2048]{1,0:T(8,128)(2,1)S(1)}, bf16[128,2048]{1,0:T(8,128)(2,1)S(1)}, u32[]{:S(2)}, u32[]{:S(2)}) collective-permute-start(bf16[128,2048]{1,0:T(8,128)(2,1)S(1)} %get-tuple-element.121), channel_id=1, source_target_pairs={{0,24},{8,0},{16,8},{24,16},{1,25},{9,1},{17,9},{25,17},{2,26},{10... | collective-permute-start | bytes 1572872 | tf_op jit(solution)/shard_map/ppermute | solution.py:16
  131.9 17.1 %collective-permute-start.9 = (bf16[4,128,2048]{2,1,0:T(8,128)(2,1)}, bf16[4,128,2048]{2,1,0:T(8,128)(2,1)}, u32[]{:S(2)}, u32[]{:S(2)}) collective-permute-start(bf16[4,128,2048]{2,1,0:T(8,128)(2,1)} %pad_maximum_fusion.1), channel_id=1, source_target_pairs={{0,4},{4,0},{1,5},{5,1},{2,6},{6,2},{3,7},{7,3},{8,12},{12,8},{9,1... | collective-permute-start | bytes 6291464 | tf_op jit(solution)/shard_map/ppermute | solution.py:44
  134.3 218.8 %reduce-scatter.4.cloned.1.call-start = ((), (), s32[]{:S(2)}) async-start(), calls=%async_computation.10 | async-start | bytes 4718592 | tf_op jit(solution)/shard_map/reduce_scatter | solution.py:351
  237.4 208.0 %all-gather.16.cloned.1.call-start = ((), (), s32[]{:S(2)}) async-start(), calls=%async_computation.14 | async-start | bytes 1179648 | tf_op jit(solution)/shard_map/all_gather | solution.py:160
  283.9 17.3 %collective-permute-start.13 = (bf16[128,2176]{0,1:T(8,128)(2,1)}, bf16[128,2176]{0,1:T(8,128)(2,1)}, u32[]{:S(2)}, u32[]{:S(2)}) collective-permute-start(bf16[128,2176]{0,1:T(8,128)(2,1)} %get-tuple-element.98), channel_id=1, source_target_pairs={{0,16},{8,24},{16,0},{24,8},{1,17},{9,25},{17,1},{25,9},{2,18},{10... | collective-permute-start | bytes 1671176 | tf_op jit(solution)/shard_map/ppermute | solution.py:16
  287.1 25.6 %collective-permute-start.12 = (bf16[128,2176]{0,1:T(8,128)(2,1)}, bf16[128,2176]{0,1:T(8,128)(2,1)}, u32[]{:S(2)}, u32[]{:S(2)}) collective-permute-start(bf16[128,2176]{0,1:T(8,128)(2,1)} %get-tuple-element.99), channel_id=1, source_target_pairs={{0,24},{8,0},{16,8},{24,16},{1,25},{9,1},{17,9},{25,17},{2,26},{10... | collective-permute-start | bytes 1671176 | tf_op jit(solution)/shard_map/ppermute | solution.py:16
  288.2 24.5 %collective-permute-start.11 = (bf16[128,2176]{0,1:T(8,128)(2,1)}, bf16[128,2176]{0,1:T(8,128)(2,1)}, u32[]{:S(2)}, u32[]{:S(2)}) collective-permute-start(bf16[128,2176]{0,1:T(8,128)(2,1)} %get-tuple-element.97), channel_id=1, source_target_pairs={{0,8},{8,16},{16,24},{24,0},{1,9},{9,17},{17,25},{25,1},{2,10},{10... | collective-permute-start | bytes 1671176 | tf_op jit(solution)/shard_map/ppermute | solution.py:16
  314.6 8.7 %collective-permute-start.16 = (bf16[128,640]{0,1:T(8,128)(2,1)S(1)}, bf16[128,640]{0,1:T(8,128)(2,1)S(1)}, u32[]{:S(2)}, u32[]{:S(2)}) collective-permute-start(bf16[128,640]{0,1:T(8,128)(2,1)S(1)} %get-tuple-element.115), channel_id=1, source_target_pairs={{0,2},{1,3},{2,0},{3,1},{4,6},{5,7},{6,4},{7,5},{8,10},{9,11},{10,... | collective-permute-start | bytes 491528 | tf_op jit(solution)/shard_map/ppermute | solution.py:16
  318.8 128.4 %all-gather.14.cloned.1.call-start = ((), (), s32[]{:S(2)}) async-start(), calls=%async_computation.13 | async-start | bytes 3538944 | tf_op jit(solution)/shard_map/all_gather | solution.py:268
  325.8 8.9 %collective-permute-start.19 = (bf16[128,512]{0,1:T(8,128)(2,1)S(1)}, bf16[128,512]{0,1:T(8,128)(2,1)S(1)}, u32[]{:S(2)}, u32[]{:S(2)}) collective-permute-start(bf16[128,512]{0,1:T(8,128)(2,1)S(1)} %slice.270), channel_id=1, source_target_pairs={{0,1},{1,2},{2,3},{3,0},{4,5},{5,6},{6,7},{7,4},{8,9},{9,10},{10,1... | collective-permute-start | bytes 393224 | tf_op jit(solution)/shard_map/ppermute | solution.py:16
  326.3 8.4 %collective-permute-start.18 = (bf16[128,512]{0,1:T(8,128)(2,1)S(1)}, bf16[128,512]{0,1:T(8,128)(2,1)S(1)}, u32[]{:S(2)}, u32[]{:S(2)}) collective-permute-start(bf16[128,512]{0,1:T(8,128)(2,1)S(1)} %slice.270), channel_id=1, source_target_pairs={{0,2},{1,3},{2,0},{3,1},{4,6},{5,7},{6,4},{7,5},{8,10},{9,11},{10,... | collective-permute-start | bytes 393224 | tf_op jit(solution)/shard_map/ppermute | solution.py:16
  347.1 134.7 %reduce-scatter.6.cloned.1.call-start = ((), (), s32[]{:S(2)}) async-start(), calls=%async_computation.11 | async-start | bytes 655360 | tf_op jit(solution)/shard_map/reduce_scatter | solution.py:354
  355.1 141.3 %reduce-scatter.8.cloned.1.call-start = ((), (), s32[]{:S(2)}) async-start(), calls=%async_computation.15 | async-start | bytes 7864320 | tf_op jit(solution)/shard_map/reduce_scatter | solution.py:348
  398.4 20.6 %all-to-all-start.2 = ((bf16[8,128,256]{1,2,0:T(8,128)(2,1)}), bf16[8,128,256]{1,2,0:T(8,128)(2,1)S(1)}, u32[]{:S(2)}, u32[]{:S(2)}) async-start(bf16[8,128,256]{1,2,0:T(8,128)(2,1)} %bitcast.84), calls=%async_computation.4 | async-start | bytes 1048576 | tf_op jit(solution)/shard_map/all_to_all | solution.py:279
  419.0 10.9 %all-to-all-start.4 = ((bf16[8,32,256]{2,1,0:T(8,128)(2,1)}), bf16[8,32,256]{2,1,0:T(8,128)(2,1)S(1)}, u32[]{:S(2)}, u32[]{:S(2)}) async-start(bf16[8,32,256]{2,1,0:T(8,128)(2,1)} %reshape.386), calls=%async_computation.6 | async-start | bytes 262144 | tf_op jit(solution)/shard_map/all_to_all | solution.py:279
  429.9 15.3 %all-to-all-start.3 = ((bf16[8,128,256]{1,2,0:T(8,128)(2,1)}), bf16[8,128,256]{1,2,0:T(8,128)(2,1)S(1)}, u32[]{:S(2)}, u32[]{:S(2)}) async-start(bf16[8,128,256]{1,2,0:T(8,128)(2,1)} %bitcast.88), calls=%async_computation.5 | async-start | bytes 1048576 | tf_op jit(solution)/shard_map/all_to_all | solution.py:279
  433.5 8.6 %collective-permute-start.22 = (bf16[128,640]{1,0:T(8,128)(2,1)S(1)}, bf16[128,640]{1,0:T(8,128)(2,1)S(1)}, u32[]{:S(2)}, u32[]{:S(2)}) collective-permute-start(bf16[128,640]{1,0:T(8,128)(2,1)S(1)} %get-tuple-element.112), channel_id=1, source_target_pairs={{0,2},{1,3},{2,0},{3,1},{4,6},{5,7},{6,4},{7,5},{8,10},{9,11},{10,... | collective-permute-start | bytes 491528 | tf_op jit(solution)/shard_map/ppermute | solution.py:16
  434.9 10.0 %collective-permute-start.21 = (bf16[128,640]{1,0:T(8,128)(2,1)S(1)}, bf16[128,640]{1,0:T(8,128)(2,1)S(1)}, u32[]{:S(2)}, u32[]{:S(2)}) collective-permute-start(bf16[128,640]{1,0:T(8,128)(2,1)S(1)} %get-tuple-element.111), channel_id=1, source_target_pairs={{0,3},{1,0},{2,1},{3,2},{4,7},{5,4},{6,5},{7,6},{8,11},{9,8},{10,9... | collective-permute-start | bytes 491528 | tf_op jit(solution)/shard_map/ppermute | solution.py:16
  436.7 8.4 %collective-permute-start.20 = (bf16[128,640]{1,0:T(8,128)(2,1)S(1)}, bf16[128,640]{1,0:T(8,128)(2,1)S(1)}, u32[]{:S(2)}, u32[]{:S(2)}) collective-permute-start(bf16[128,640]{1,0:T(8,128)(2,1)S(1)} %get-tuple-element.110), channel_id=1, source_target_pairs={{0,1},{1,2},{2,3},{3,0},{4,5},{5,6},{6,7},{7,4},{8,9},{9,10},{10,1... | collective-permute-start | bytes 491528 | tf_op jit(solution)/shard_map/ppermute | solution.py:16
  450.3 17.1 %collective-permute-start.28 = (bf16[64,2176]{1,0:T(8,128)(2,1)S(1)}, bf16[64,2176]{1,0:T(8,128)(2,1)S(1)}, u32[]{:S(2)}, u32[]{:S(2)}) collective-permute-start(bf16[64,2176]{1,0:T(8,128)(2,1)S(1)} %get-tuple-element.105), channel_id=1, source_target_pairs={{0,64},{32,96},{64,0},{96,32},{1,65},{33,97},{65,1},{97,33},{2,66}... | collective-permute-start | bytes 835592 | tf_op jit(solution)/shard_map/ppermute | solution.py:16
  453.4 25.7 %collective-permute-start.27 = (bf16[64,2176]{1,0:T(8,128)(2,1)S(1)}, bf16[64,2176]{1,0:T(8,128)(2,1)S(1)}, u32[]{:S(2)}, u32[]{:S(2)}) collective-permute-start(bf16[64,2176]{1,0:T(8,128)(2,1)S(1)} %get-tuple-element.106), channel_id=1, source_target_pairs={{0,96},{32,0},{64,32},{96,64},{1,97},{33,1},{65,33},{97,65},{2,98}... | collective-permute-start | bytes 835592 | tf_op jit(solution)/shard_map/ppermute | solution.py:16
  454.5 24.6 %collective-permute-start.26 = (bf16[64,2176]{1,0:T(8,128)(2,1)S(1)}, bf16[64,2176]{1,0:T(8,128)(2,1)S(1)}, u32[]{:S(2)}, u32[]{:S(2)}) collective-permute-start(bf16[64,2176]{1,0:T(8,128)(2,1)S(1)} %get-tuple-element.104), channel_id=1, source_target_pairs={{0,32},{32,64},{64,96},{96,0},{1,33},{33,65},{65,97},{97,1},{2,34}... | collective-permute-start | bytes 835592 | tf_op jit(solution)/shard_map/ppermute | solution.py:16
  483.5 11.9 %all-to-all-start.1 = ((bf16[8,16,1024]{2,1,0:T(8,128)(2,1)}), bf16[8,16,1024]{2,1,0:T(8,128)(2,1)S(1)}, u32[]{:S(2)}, u32[]{:S(2)}) async-start(bf16[8,16,1024]{2,1,0:T(8,128)(2,1)} %bitcast.81), calls=%async_computation.3 | async-start | bytes 524288 | tf_op jit(solution)/shard_map/all_to_all | solution.py:363
  (50 other events, 381.5 us)
Sparse Core Ops, SparseCore 0:
  12.3 59.9 all-gather.7
  74.5 23.0 all-gather.17
  99.3 65.4 all-gather.9
  166.9 48.9 all-gather.11
  237.5 38.5 reduce-scatter.3
  318.9 24.1 all-gather.15
  347.3 32.8 all-gather.13
  383.1 22.2 reduce-scatter.5
  407.8 75.5 reduce-scatter.7
